TPU v7x, 256 devices: a whole 4x4x8 slice. The times are simulated.
256 devices in a mesh: dp: 64 (over z, x_lo, y), mp: 4 (over x_hi, core).
Axes of the slice: x: 4 (x_hi: 2, x_lo: 2; x = x_hi * 2 + x_lo), y: 4, z: 8, core: 2. Of those that a mesh axis runs over, the one named last changes fastest.
Arguments:
- image_feats: bfloat16 [8704, 1536], P('dp'), may hold values from -16 to 16
- text_feats: bfloat16 [8704, 1152], P('dp'), may hold values from -16 to 16
- image_head: bfloat16 [1536, 1536], P(None, 'mp'), may hold values from -0.15625 to 0.15625
- text_head: bfloat16 [1152, 1536], P(None, 'mp'), may hold values from -0.1875 to 0.1875
- log_temp: float32 [1], replicated, may hold values from 1.5 to 2.5
- logit_bias: float32 [1], replicated, may hold values from -4 to -1
Outputs:
- image_head_grad: float32 [1536, 1536], P('dp', 'mp')
- text_head_grad: float32 [1152, 1536], P('dp', 'mp')
All inputs are finite; a program needn't handle non-finite values.
Results may differ from a plain program's by a relative error of at most 0.004.
Values may be sent and summed in bfloat16 or wider, within the bound.
A program may use at most 128 MiB of HBM per device.

v0:
```python
import jax
import jax.numpy as jnp
from jax import lax
from jax.sharding import PartitionSpec as P


def pair_grads(summed, row_ids, column_ids, temper, logit_bias):
    logits = temper * summed + logit_bias[0]
    return (temper * (jax.nn.sigmoid(logits) - (column_ids == row_ids).astype(jnp.float32))).astype(
        jnp.bfloat16
    )


def body(image_feats, text_feats, image_head, text_head, log_temp, logit_bias):
    row_count = image_feats.shape[0]
    img_pre = jnp.dot(image_feats, image_head, preferred_element_type=jnp.float32)
    txt_pre = jnp.dot(text_feats, text_head, preferred_element_type=jnp.float32)
    img_sq, txt_sq = lax.psum(
        (jnp.sum(img_pre * img_pre, axis=1), jnp.sum(txt_pre * txt_pre, axis=1)), "mp"
    )
    img_norm = jnp.sqrt(img_sq + 1e-06)
    txt_norm = jnp.sqrt(txt_sq + 1e-06)
    img_dir = img_pre / img_norm[:, None]
    txt_dir = txt_pre / txt_norm[:, None]
    img_unit = img_dir.astype(jnp.bfloat16)
    txt_unit = txt_dir.astype(jnp.bfloat16)
    temper = jnp.exp(log_temp[0])
    offset = lax.axis_index("dp") * row_count
    row_ids = offset + jnp.arange(row_count, dtype=jnp.int32)[:, None]
    contract = (((1,), (1,)), ((), ()))
    all_texts = lax.all_gather(txt_unit, "dp", axis=0, tiled=True)
    partial_value = lax.dot_general(
        img_unit, all_texts, contract, preferred_element_type=jnp.float32
    )
    column_ids = jnp.arange(all_texts.shape[0], dtype=jnp.int32)[None, :]
    summed = lax.psum(partial_value, "mp")
    pair_grad = pair_grads(summed, row_ids, column_ids, temper, logit_bias)
    img_unit_grad = jnp.dot(pair_grad, all_texts, preferred_element_type=jnp.float32)
    text_part = lax.psum_scatter(
        lax.dot_general(
            pair_grad, img_unit, (((0,), (0,)), ((), ())), preferred_element_type=jnp.float32
        ),
        "dp",
        scatter_dimension=0,
        tiled=True,
    )
    img_along, txt_along = lax.psum(
        (jnp.sum(img_unit_grad * img_dir, axis=1), jnp.sum(text_part * txt_dir, axis=1)), "mp"
    )
    img_grad = ((img_unit_grad - img_dir * img_along[:, None]) / img_norm[:, None]).astype(
        jnp.bfloat16
    )
    txt_grad = ((text_part - txt_dir * txt_along[:, None]) / txt_norm[:, None]).astype(jnp.bfloat16)
    img_term = lax.dot_general(
        image_feats, img_grad, (((0,), (0,)), ((), ())), preferred_element_type=jnp.float32
    )
    txt_term = lax.dot_general(
        text_feats, txt_grad, (((0,), (0,)), ((), ())), preferred_element_type=jnp.float32
    )
    image_head_grad, text_head_grad = (
        lax.psum_scatter(img_term, "dp", scatter_dimension=0, tiled=True),
        lax.psum_scatter(txt_term, "dp", scatter_dimension=0, tiled=True),
    )
    return (image_head_grad, text_head_grad)


def solution(mesh):
    placed = (P("dp", None), P("dp", None), P(None, "mp"), P(None, "mp"), P(), P())
    return jax.shard_map(
        body, mesh=mesh, in_specs=placed, out_specs=(P("dp", "mp"), P("dp", "mp")), check_vma=False
    )
```

profile of v0, /device:TPU:4, one launch (start us, length us, event | category | flops | bytes accessed | tf_op | source)
XLA Modules:
  0.0 1440.9 jit_solution(14958864801441692113)
XLA Ops:
  7.2 1.2 copy-done
  8.4 1.5 multiply_reduce_fusion.3
  9.9 1.7 multiply_reduce_fusion.2
  11.7 7.2 all-reduce.5
  18.9 0.7 fusion.8
  19.6 0.0 all-reduce.9.cloned.1.call-start
  19.7 313.3 %all-gather.2.cloned.1.call-done = bf16[8704,384]{1,0:T(8,128)(2,1)} async-done(((bf16[136,384]{1,0:T(8,128)(2,1)}), bf16[8704,384]{1,0:T(8,128)(2,1)}) %all-gather.2.cloned.1.call-update) | async-done | bytes 6684688 | tf_op jit(solution)/shard_map/all_gather | solution.py:31
  333.0 8.0 fusion.6
  341.0 0.0 reduce-scatter.7.cloned.1.call-start
  342.4 99.8 %all-reduce.9.cloned.1.call-done = f32[136,8704]{1,0:T(8,128)} async-done(((f32[136,8704]{1,0:T(8,128)}), f32[136,8704]{1,0:T(8,128)}) %all-reduce.9.cloned.1.call-update) | async-done | bytes 4734992 | tf_op jit(solution)/shard_map/psum | solution.py:36
  442.3 10.3 fusion.4
  452.6 0.0 all-reduce.11.cloned.1.call-start
  452.7 6.8 multiply_reduce_fusion.1
  459.5 343.5 %reduce-scatter.7.cloned.1.call-done = f32[136,384]{1,0:T(8,128)} async-done(((f32[8704,384]{1,0:T(8,128)}), f32[136,384]{1,0:T(8,128)}) %reduce-scatter.7.cloned.1.call-update) | async-done | bytes 208912
  803.0 1.1 multiply_reduce_fusion
  804.2 7.3 all-reduce.4
  811.4 2.0 convolution_bitcast_fusion.1
  813.4 2.7 convolution_bitcast_fusion
  816.2 0.6 dynamic-slice
  818.1 612.6 %all-reduce.11.cloned.1.call-done = (f32[1536,384]{0,1:T(8,128)}, f32[1152,384]{0,1:T(8,128)}) async-done(((f32[1536,384]{0,1:T(8,128)}, f32[1152,384]{0,1:T(8,128)}), (f32[1536,384]{0,1:T(8,128)}, f32[1152,384]{0,1:T(8,128)})) %all-reduce.11.cloned.1.call-update) | async-done | bytes 4128784
  1430.7 1.1 constant_dynamic-slice_fusion.1
  1431.8 0.7 copy.10
  1432.5 1.1 constant_dynamic-slice_fusion
  1433.6 0.7 copy.11
  (15 shorter events, 0.1 us)
Async XLA Ops:
  7.2 1.3 copy-start
  7.2 325.8 %all-gather.2.cloned.1.call-start = ((), (), s32[]{:S(2)}) async-start(), calls=%async_computation.1 | async-start | bytes 6789120 | tf_op jit(solution)/shard_map/all_gather | solution.py:31
  19.6 422.6 %all-reduce.9.cloned.1.call-start = ((), (), s32[]{:S(2)}) async-start(), calls=%async_computation.2 | async-start | bytes 9469952 | tf_op jit(solution)/shard_map/psum | solution.py:36
  341.0 462.0 %reduce-scatter.7.cloned.1.call-start = ((), (), s32[]{:S(2)}) async-start(), calls=%async_computation.3 | async-start | bytes 13578240
  452.6 978.1 %all-reduce.11.cloned.1.call-start = ((), (), s32[]{:S(2)}) async-start(), calls=%async_computation.4 | async-start | bytes 8257536
  452.7 358.8 %copy-start.1 = (bf16[136,1536]{1,0:T(8,128)(2,1)S(1)}, bf16[136,1536]{1,0:T(8,128)(2,1)}, u32[]{:S(2)}) copy-start(bf16[136,1536]{1,0:T(8,128)(2,1)} %param.6) | copy-start | bytes 1253380
  452.7 360.8 %copy-start.2 = (bf16[136,1152]{1,0:T(8,128)(2,1)S(1)}, bf16[136,1152]{1,0:T(8,128)(2,1)}, u32[]{:S(2)}) copy-start(bf16[136,1152]{1,0:T(8,128)(2,1)} %param.7) | copy-start | bytes 940036
  811.4 4.8 copy-start.3
Sparse Core Ops, SparseCore 0:
  19.7 313.1 all-gather.1
  341.1 101.0 all-reduce.8
  452.7 350.2 reduce-scatter.6
  816.3 614.3 all-reduce.10
where the time goes:
time: 1440 us
  waiting for transfers between devices  1370 us (95%)
  matrix products  33.1 us (2%)
  between operations  16.5 us (1%)
  blocking collectives  14.5 us (1%)
    unnamed x6, waiting for transfers between devices  956 us
    all_gather x1, waiting for transfers between devices, body(): all_texts = lax.all_gather(txt_unit, 'dp', axis=0, tiled=True)  313 us
    psum x1, waiting for transfers between devices, body(): summed = lax.psum(partial_value, 'mp')  99.8 us
  transfers between devices with their start and end apart: 4, of which 4 were waited for; matrix products, arithmetic and copies ran while one was open for 1% of the time, Pallas kernels for 0%

commit v1 on v0

v1 whole, which is shorter than its diff:
```python
import jax
import jax.numpy as jnp
from jax import lax
from jax.experimental import pallas as pl
from jax.experimental.pallas import tpu as pltpu
from jax.sharding import PartitionSpec as P

F32 = jnp.float32
BF16 = jnp.bfloat16
MESH = pl.DeviceIdType.MESH
NT = (((1,), (1,)), ((), ()))
TN = (((0,), (0,)), ((), ()))
NN = (((1,), (0,)), ((), ()))
R = 136
RT = 144
RI = 80
W = 384
MESSAGES = 160


def kernel(
    xf, tf, xh_ref, th_ref, log_temp, logit_bias, out_i, out_t,
    sums, norm_b, dir_t, dir_i, parts, texts, images, mine, theirs, pg, grad_i, grad_t, grad_tb,
    ring_s, ring_r, half_s, half_r, ta_r, tb_r, ta_sum, tb_sum, ta_s, tb_s, ta_r2, tb_r2,
    along, head_t, head_i, ht_s0, ht_r0, ht_s1, ht_r1, xt, xt_r, si, ri, zi, zi_r,
    send_sem, recv_sem,
):
    dp, mp = lax.axis_index("dp"), lax.axis_index("mp")
    z, xl, y = lax.div(dp, 8), lax.rem(lax.div(dp, 4), 2), lax.rem(dp, 4)
    xh, core = lax.div(mp, 2), lax.rem(mp, 2)
    x = xh * 2 + xl

    def at(z_at=None, x_at=None, y_at=None, core_at=None):
        z_at = z if z_at is None else z_at
        x_at = x if x_at is None else x_at
        y_at = y if y_at is None else y_at
        core_at = core if core_at is None else core_at
        return (
            (z_at * 2 + lax.rem(x_at, 2)) * 4 + y_at,
            lax.div(x_at, 2) * 2 + core_at,
        )

    def zo(o):
        return lax.rem(z + o + 8, 8)

    def xo(o):
        return lax.rem(x + o + 4, 4)

    def yo(o):
        return lax.rem(y + o + 4, 4)

    started = []

    def message(src, dst, where):
        k = len(started)
        copy = pltpu.make_async_remote_copy(
            src_ref=src, dst_ref=dst, send_sem=send_sem.at[k], recv_sem=recv_sem.at[k],
            device_id=where, device_id_type=MESH,
        )
        copy.start()
        started.append(copy)
        return copy

    def lanes(half):
        return pl.ds(pl.multiple_of(half * W, 128), W)

    barrier = pltpu.get_barrier_semaphore()
    peers = [at(x_at=xo(a), y_at=yo(b)) for a in range(4) for b in range(4) if a or b]
    peers += [at(z_at=zo(o)) for o in range(1, 8)]
    peers += [at(core_at=1 - core), at(x_at=xo(2), core_at=1 - core)]
    for peer in peers:
        pl.semaphore_signal(barrier, inc=1, device_id=peer, device_id_type=MESH)

    def padded(value, rows):
        return jnp.concatenate([value, jnp.zeros((rows - value.shape[0],) + value.shape[1:], value.dtype)], axis=0)

    txt_pre = jnp.dot(tf[...], th_ref[...], preferred_element_type=F32)
    dir_t[...] = padded(txt_pre, RT)
    img_pre = jnp.dot(xf[...], xh_ref[...], preferred_element_type=F32)
    dir_i[...] = padded(img_pre, RT)
    left = lax.broadcasted_iota(jnp.int32, (RT, 128), 1) < 64

    def two_sums(a, b):
        return jnp.where(left, jnp.sum(a, axis=1, keepdims=True), jnp.sum(b, axis=1, keepdims=True))

    def over_mp(ref, value):
        ref[mp] = value
        got = [
            message(ref.at[mp], ref.at[mp], where)
            for where in (at(core_at=1 - core), at(x_at=xo(2)), at(x_at=xo(2), core_at=1 - core))
        ]
        for copy in got:
            copy.wait_recv()
        return (ref[0] + ref[1]) + (ref[2] + ref[3])

    a, b = dir_t[...], dir_i[...]
    value = two_sums(a * a, b * b)
    pl.semaphore_wait(barrier, len(peers))
    norms = jnp.sqrt(over_mp(sums, value) + 1e-06)
    txt_norm, img_norm = norms[:, 0:1], norms[:, 64:65]
    txt_dir = dir_t[...] / txt_norm
    img_dir = dir_i[...] / img_norm
    dir_t[...] = txt_dir
    dir_i[...] = img_dir
    norm_b[...] = norms

    slot = xl * 4 + y
    own, other = lanes(xh), lanes(1 - xh)
    texts[slot, :, own] = txt_dir.astype(BF16)
    low, high = pl.ds(0, 64), pl.ds(64, 80)
    stage_a = [message(texts.at[slot, low, own], texts.at[slot, low, own], at(x_at=xo(o))) for o in (1, 2, 3)]
    stage_b = [message(texts.at[slot, high, own], texts.at[slot, high, own], at(y_at=yo(o))) for o in (1, 2, 3)]
    parts[0] = padded(img_dir[0:64], RI).astype(BF16)
    parts[1] = img_dir[64:144].astype(BF16)
    swap = message(parts.at[1 - xh], images.at[z, :, own], at(x_at=xo(2)))
    images[z, :, own] = parts[xh]
    up, down = at(z_at=zo(1)), at(z_at=zo(-1))
    kinds = (own, other)
    ups, downs = {}, {}
    for q in (0, 1):
        if q == 1:
            swap.wait_recv()
        ups[q, 1] = message(images.at[z, :, kinds[q]], images.at[z, :, kinds[q]], up)
        downs[q, 1] = message(images.at[z, :, kinds[q]], images.at[z, :, kinds[q]], down)

    def pass_images(step):
        for q in (0, 1):
            if (q, step) in ups:
                ups[q, step].wait_recv()
                if step < 4 - q:
                    view = images.at[zo(-step), :, kinds[q]]
                    ups[q, step + 1] = message(view, view, up)
            if (q, step) in downs:
                downs[q, step].wait_recv()
                if step < 3 + q:
                    view = images.at[zo(step), :, kinds[q]]
                    downs[q, step + 1] = message(view, view, down)

    for copy in stage_a:
        copy.wait_recv()
    stage_a2 = []
    for o in (1, 2, 3):
        for k in (0, 1):
            view = texts.at[k * 4 + y, low, :]
            stage_a2.append(message(view, view, at(y_at=yo(o))))
    for copy in stage_b:
        copy.wait_recv()
    stage_b2 = []
    for o in (1, 2, 3):
        for k in range(4):
            view = texts.at[xl * 4 + k, high, own]
            stage_b2.append(message(view, view, at(x_at=xo(o))))
    for step in (1, 2, 3, 4):
        pass_images(step)
    for copy in stage_a2 + stage_b2:
        copy.wait_recv()

    all_texts = texts[...].reshape(8 * RT, 2 * W)
    theirs_at = pl.ds((1 - core) * 4, 4)
    mine_at = pl.ds(core * 4, 4)
    theirs[...] = lax.dot_general(
        images[theirs_at].reshape(4 * RI, 2 * W), all_texts, NT, preferred_element_type=F32
    ).reshape(4, RI, 8 * RT)
    cross = message(theirs, mine.at[1], at(core_at=1 - core))
    mine[0] = lax.dot_general(
        images[mine_at].reshape(4 * RI, 2 * W), all_texts, NT, preferred_element_type=F32
    ).reshape(4, RI, 8 * RT)
    cross.wait_recv()
    temper = jnp.exp(jnp.full((1, 128), log_temp[0], F32))[:, 0:1]
    bias = logit_bias[0]
    ahead = lax.broadcasted_iota(jnp.int32, (RI, 8 * RT), 1) - lax.broadcasted_iota(jnp.int32, (RI, 8 * RT), 0)

    @pl.loop(0, 4)
    def _(block):
        logits = temper * (mine[0, block] + mine[1, block]) + bias
        same = ahead == jnp.where(core * 4 + block == z, slot * RT + 64 * xh, -8192)
        pg[core * 4 + block] = (temper * (jax.nn.sigmoid(logits) - same.astype(F32))).astype(BF16)

    share = message(pg.at[mine_at], pg.at[mine_at], at(core_at=1 - core))
    share.wait_recv()
    every = pg[...].reshape(8 * RI, 8 * RT)
    grad_i[...] = lax.dot_general(every, all_texts, NN, preferred_element_type=F32).reshape(8, RI, 2 * W)
    grad_t[...] = lax.dot_general(
        every, images[...].reshape(8 * RI, 2 * W), TN, preferred_element_type=F32
    ).reshape(8, RT, 2 * W)

    grad_tb[...] = grad_t[...].astype(BF16)
    back_a, back_b = {}, {}
    for o in (1, 2, 3):
        for k in (0, 1):
            back_a[o, k] = message(grad_tb.at[k * 4 + yo(o), low, :], ta_r.at[o - 1, k], at(y_at=yo(o)))
    for o in (1, 2, 3):
        to = xo(o)
        for k in range(4):
            back_b[o, k] = message(
                grad_tb.at[lax.rem(to, 2) * 4 + k, high, lanes(lax.div(to, 2))], tb_r.at[o - 1, k], at(x_at=to)
            )

    def ring(piece, send, recv, chain, finish):
        went = {}
        for step in (1, 2, 3, 4):
            for q in (0, 1):
                for way, sign, length in ((0, 1, chain[q]), (1, -1, 7 - chain[q])):
                    first = 5 - length
                    if step < first:
                        continue
                    value = piece(q, zo(sign * (5 - step)))
                    if step > first:
                        went[way, q, step - 1].wait_recv()
                        value = value + recv(q, way, step - 1)[...].astype(F32)
                    send(q, way, step)[...] = value.astype(BF16)
                    went[way, q, step] = message(
                        send(q, way, step), recv(q, way, step), at(z_at=zo(sign))
                    )
        for q in (0, 1):
            total = piece(q, z)
            for way in (0, 1):
                went[way, q, 4].wait_recv()
                total = total + recv(q, way, 4)[...].astype(F32)
            finish(q, total)

    def image_done(q, total):
        if q == 0:
            dir_own[...] = total
        else:
            half_s[...] = total.astype(BF16)

    dir_own = mine.at[0, 0, :, pl.ds(0, W)]
    ring(
        lambda q, to: grad_i[to, :, kinds[q]],
        lambda q, way, step: ring_s.at[q, way, step - 1],
        lambda q, way, step: ring_r.at[q, way, step - 1],
        (4, 3),
        image_done,
    )
    swap_back = message(half_s, half_r, at(x_at=xo(2)))

    for copy in back_a.values():
        copy.wait_recv()
    for k in (0, 1):
        ta_sum[k] = grad_t[k * 4 + y, low, :] + sum(ta_r[o, k].astype(F32) for o in range(3))
    ta_s[...] = ta_sum[...].astype(BF16)
    back_a2 = []
    for o in (1, 2, 3):
        to = xo(o)
        back_a2.append(message(ta_s.at[lax.rem(to, 2), :, lanes(lax.div(to, 2))], ta_r2.at[o - 1], at(x_at=to)))
    for copy in back_b.values():
        copy.wait_recv()
    for k in range(4):
        tb_sum[k] = grad_t[xl * 4 + k, high, own] + sum(tb_r[o, k].astype(F32) for o in range(3))
    tb_s[...] = tb_sum[...].astype(BF16)
    back_b2 = [message(tb_s.at[yo(o)], tb_r2.at[o - 1], at(y_at=yo(o))) for o in (1, 2, 3)]
    for copy in back_a2 + back_b2:
        copy.wait_recv()
    txt_unit_grad = jnp.concatenate(
        [
            ta_sum[xl, :, own] + sum(ta_r2[o].astype(F32) for o in range(3)),
            tb_sum[y] + sum(tb_r2[o].astype(F32) for o in range(3)),
        ],
        axis=0,
    )
    swap_back.wait_recv()
    grad_i[xh, :, pl.ds(0, W)] = dir_own[...]
    grad_i[1 - xh, :, pl.ds(0, W)] = half_r[...].astype(F32)
    img_unit_grad = jnp.concatenate([grad_i[0, pl.ds(0, 64), pl.ds(0, W)], grad_i[1, :, pl.ds(0, W)]], axis=0)

    txt_dir, img_dir, norms = dir_t[...], dir_i[...], norm_b[...]
    alongs = over_mp(along, two_sums(txt_unit_grad * txt_dir, img_unit_grad * img_dir))
    txt_grad = ((txt_unit_grad - txt_dir * alongs[:, 0:1]) / norms[:, 0:1]).astype(BF16)
    img_grad = ((img_unit_grad - img_dir * alongs[:, 64:65]) / norms[:, 64:65]).astype(BF16)

    head_i[...] = lax.dot_general(xf[...], img_grad[0:R], TN, preferred_element_type=F32)
    for j in range(8):
        si[j] = jnp.concatenate([head_i[pl.ds(k * 192 + j * 24, 24), :] for k in range(8)], axis=0).astype(BF16)
    out_xy = {}
    for a in (0, 1):
        for b in range(4):
            if a or b:
                to_xl = lax.rem(xl + a, 2)
                out_xy[a, b] = message(
                    si.at[to_xl * 4 + yo(b)], ri.at[a * 4 + b - 1], at(x_at=xh * 2 + to_xl, y_at=yo(b))
                )
    head_t[...] = lax.dot_general(tf[...], txt_grad[0:R], TN, preferred_element_type=F32)
    sends, recvs = (ht_s0, ht_s1), (ht_r0, ht_r1)
    spans = ((0, 64), (64, 80))

    def text_done(q, total):
        head_t[pl.ds(spans[q][0], spans[q][1]), :] = total

    ring(
        lambda q, to: head_t[pl.ds(pl.multiple_of(to * 144 + spans[q][0], 16), spans[q][1]), :],
        lambda q, way, step: sends[q].at[way, step - 1],
        lambda q, way, step: recvs[q].at[way, step - 1],
        (4, 3),
        text_done,
    )
    total = head_t[pl.ds(0, 144), :]
    for j in range(8):
        xt[j] = padded(total[18 * j : 18 * j + 18], 24)
    last_t = []
    for a in (0, 1):
        for b in range(4):
            if a or b:
                to_xl = lax.rem(xl + a, 2)
                last_t.append(
                    message(xt.at[to_xl * 4 + yo(b)], xt_r.at[a * 4 + b - 1], at(x_at=xh * 2 + to_xl, y_at=yo(b)))
                )
    for copy in out_xy.values():
        copy.wait_recv()
    for k in range(8):
        zi[k] = head_i[pl.ds(pl.multiple_of(k * 192 + slot * 24, 8), 24), :]
    for j in range(7):
        zi[...] = zi[...] + ri[j].astype(F32).reshape(8, 24, W)
    last_i = [message(zi.at[zo(o)], zi_r.at[o - 1], at(z_at=zo(o))) for o in range(1, 8)]
    for copy in last_t:
        copy.wait_recv()
    out_t[...] = (xt[slot] + sum(xt_r[j] for j in range(7)))[0:18]
    for copy in last_i:
        copy.wait_recv()
    out_i[...] = zi[z] + sum(zi_r[j] for j in range(7))
    for copy in started:
        copy.wait_send()


def body(image_feats, text_feats, image_head, text_head, log_temp, logit_bias):
    vmem = pl.BlockSpec(memory_space=pltpu.VMEM)
    smem = pl.BlockSpec(memory_space=pltpu.SMEM)

    def f32(*shape):
        return pltpu.VMEM(shape, F32)

    def bf16(*shape):
        return pltpu.VMEM(shape, BF16)

    scratch = [
        f32(4, RT, 128), f32(RT, 128), f32(RT, W), f32(RT, W),
        bf16(2, RI, W), bf16(8, RT, 2 * W), bf16(8, RI, 2 * W),
        f32(2, 4, RI, 8 * RT), f32(4, RI, 8 * RT), bf16(8, RI, 8 * RT),
        f32(8, RI, 2 * W), f32(8, RT, 2 * W), bf16(8, RT, 2 * W),
        bf16(2, 2, 4, RI, W), bf16(2, 2, 4, RI, W), bf16(RI, W), bf16(RI, W),
        bf16(3, 2, 64, 2 * W), bf16(3, 4, 80, W), f32(2, 64, 2 * W), f32(4, 80, W),
        bf16(2, 64, 2 * W), bf16(4, 80, W), bf16(3, 64, W), bf16(3, 80, W),
        f32(4, RT, 128), f32(1152, W), f32(1536, W),
        bf16(2, 4, 64, W), bf16(2, 4, 64, W), bf16(2, 4, 80, W), bf16(2, 4, 80, W),
        f32(8, 24, W), f32(7, 24, W), bf16(8, 192, W), bf16(7, 192, W), f32(8, 24, W), f32(7, 24, W),
        pltpu.SemaphoreType.DMA((MESSAGES,)), pltpu.SemaphoreType.DMA((MESSAGES,)),
    ]
    return pl.pallas_call(
        kernel,
        out_shape=(jax.ShapeDtypeStruct((24, W), F32), jax.ShapeDtypeStruct((18, W), F32)),
        in_specs=[vmem, vmem, vmem, vmem, smem, smem],
        out_specs=(vmem, vmem),
        scratch_shapes=scratch,
        compiler_params=pltpu.CompilerParams(
            collective_id=0, has_side_effects=True, vmem_limit_bytes=56 * 1024 * 1024
        ),
        name="pair_loss",
    )(image_feats, text_feats, image_head, text_head, log_temp, logit_bias)


def solution(mesh):
    placed = (P("dp", None), P("dp", None), P(None, "mp"), P(None, "mp"), P(), P())
    return jax.shard_map(
        body, mesh=mesh, in_specs=placed, out_specs=(P("dp", "mp"), P("dp", "mp")), check_vma=False
    )
```

time: 1440 us -> 110 us (0.08)
  the two profiles are of different devices: /device:TPU:4 before, /device:TPU:1 now
where the time goes in v1:
time: 110 us
  Pallas kernels  105 us (95%)
  local copies, waits for them, and re-layouts  2.77 us (3%)
  between operations  1.93 us (2%)
    pallas_call x1, Pallas kernels, body(): pl.pallas_call(kernel, out_shape=(jax.ShapeDtypeStruct((24, W), F32), jax...  105 us
    unnamed x2, local copies, waits for them, and re-layouts  2.77 us

profile of v1, /device:TPU:1, one launch (start us, length us, event | category | flops | bytes accessed | tf_op | source)
XLA Modules:
  0.0 109.7 jit_solution(11811194851546332014)
XLA Ops:
  1.9 105.0 %pair_loss.1 = (f32[24,384]{1,0:T(8,128)}, f32[18,384]{1,0:T(8,128)}) custom-call(bf16[136,1536]{1,0:T(8,128)(2,1)} %xf.1, bf16[136,1152]{1,0:T(8,128)(2,1)} %tf.1, bf16[1536,384]{1,0:T(8,128)(2,1)} %xh_ref.1, bf16[1152,384]{1,0:T(8,128)(2,1)} %th_ref.1, f32[1]{0:T(128)S(6)} %copy.10.log_temp, f32[1]{0:T(128)S(6)} %copy.11.logit_bias), custom_call_target="tpu_custom_call" | custom-call | tf_op jit(solution)/shard_map/pair_loss/pallas_call | solution.py:348
  106.9 1.4 %copy.12 = f32[24,384]{1,0:T(8,128)} copy(f32[24,384]{1,0:T(8,128)} %get-tuple-element.4) | data formatting | bytes 73728
  108.3 1.4 %copy.13 = f32[18,384]{1,0:T(8,128)} copy(f32[18,384]{1,0:T(8,128)} %get-tuple-element.5) | data formatting | bytes 55296

commit v2 on v0

v2 whole, which is shorter than its diff:
```python
import types

import jax
import jax.numpy as jnp
from jax import lax
from jax.experimental import pallas as pl
from jax.experimental.pallas import tpu as pltpu
from jax.sharding import PartitionSpec as P

F32 = jnp.float32
BF16 = jnp.bfloat16
MESH = pl.DeviceIdType.MESH
NT = (((1,), (1,)), ((), ()))
TN = (((0,), (0,)), ((), ()))
NN = (((1,), (0,)), ((), ()))
R = 136
RT = 144
RI = 80
W = 384
MESSAGES = 200
RA, RB = 64, 80
I_CHUNKS = ((0, (0, 48)), (0, (48, 32)), (1, (0, 48)), (1, (48, 32)))
T_CHUNKS = ((0, 32), (32, 32), (64, 32), (96, 48))


def f32(*shape):
    return pltpu.VMEM(shape, F32)


def bf16(*shape):
    return pltpu.VMEM(shape, BF16)


def scratch_of():
    made = dict(
        xf=bf16(R, 1536), tf=bf16(R, 1152), xh=bf16(1536, W), th=bf16(1152, W),
        sums_t=f32(4, 8, 256), sums_i=f32(4, 8, 256), along_t=f32(4, 8, 256), along_i=f32(4, 8, 256),
        norm_t=f32(RT, 128), norm_i=f32(RT, 128), dir_t=f32(RT, W), dir_i=f32(RT, W),
        parts=bf16(2, RI, W), texts_a=bf16(2, 4, RA, 2 * W), texts_b=bf16(2, 4, RB, 2 * W), images=bf16(8, RI, 2 * W),
        mine_a=f32(4, RI, 8 * RA), theirs_a=f32(4, RI, 8 * RA), got_a=f32(4, RI, 8 * RA), pg_a=bf16(8, RI, 8 * RA),
        mine_b=f32(4, RI, 8 * RB), theirs_b=f32(4, RI, 8 * RB), got_b=f32(4, RI, 8 * RB), pg_b=bf16(8, RI, 8 * RB),
        grad_i=f32(8, RI, 2 * W), grad_a=f32(2, 4, RA, 2 * W), grad_b=f32(2, 4, RB, 2 * W),
        grad_as=bf16(2, 4, RA, 2 * W), grad_bs=bf16(2, 4, RB, 2 * W),
        a1=bf16(3, 2, RA, 2 * W), a_sum=f32(2, RA, 2 * W), a_s=bf16(2, RA, 2 * W), a2=bf16(3, RA, W),
        b1=bf16(3, 4, RB, W), b_sum=f32(4, RB, W), b_s=bf16(4, RB, W), b2=bf16(3, RB, W),
        swap_s=bf16(RI, W), swap_r=bf16(RI, W), both=f32(2, RI, W), t_sum=f32(RT, W),
        head_t=f32(1152, W), head_i=f32(1536, W), si=bf16(8, 192, W), ri=bf16(7, 192, W),
        zi=f32(8, 24, W), zi_s=bf16(8, 32, W), zi_r=bf16(7, 32, W), xt=f32(8, 24, W), xt_r=f32(7, 24, W),
    )

    def ring(name, steps, *shapes):
        for q, shape in enumerate(shapes):
            made[f"{name}_s{q}"] = bf16(2, steps, *shape)
            made[f"{name}_r{q}"] = bf16(2, steps, *shape)

    ring("img", 4, *((n, W) for _, (_, n) in I_CHUNKS))
    ring("ht", 4, *((n, W) for _, n in T_CHUNKS))
    made.update(
        send_sem=pltpu.SemaphoreType.DMA((MESSAGES,)),
        recv_sem=pltpu.SemaphoreType.DMA((MESSAGES,)),
        load_sem=pltpu.SemaphoreType.DMA((4,)),
    )
    return made


def kernel(names, xf_any, tf_any, xh_any, th_any, log_temp, logit_bias, out_i, out_t, *refs):
    s = types.SimpleNamespace(**dict(zip(names, refs)))
    dp, mp = lax.axis_index("dp"), lax.axis_index("mp")
    z, xl, y = lax.div(dp, 8), lax.rem(lax.div(dp, 4), 2), lax.rem(dp, 4)
    xh, core = lax.div(mp, 2), lax.rem(mp, 2)
    x = xh * 2 + xl
    slot = xl * 4 + y

    def at(z_at=None, x_at=None, y_at=None, core_at=None):
        z_at = z if z_at is None else z_at
        x_at = x if x_at is None else x_at
        y_at = y if y_at is None else y_at
        core_at = core if core_at is None else core_at
        return (
            (z_at * 2 + lax.rem(x_at, 2)) * 4 + y_at,
            lax.div(x_at, 2) * 2 + core_at,
        )

    def zo(o):
        return lax.rem(z + o + 8, 8)

    def xo(o):
        return lax.rem(x + o + 4, 4)

    def yo(o):
        return lax.rem(y + o + 4, 4)

    def to_z(o):
        return at(z_at=zo(o))

    def to_x(o):
        return at(x_at=xo(o))

    def to_y(o):
        return at(y_at=yo(o))

    across = at(x_at=xh * 2 + 1 - xl)
    twin = at(core_at=1 - core)

    started = []

    def message(src, dst, where):
        k = len(started)
        copy = pltpu.make_async_remote_copy(
            src_ref=src, dst_ref=dst, send_sem=s.send_sem.at[k], recv_sem=s.recv_sem.at[k],
            device_id=where, device_id_type=MESH,
        )
        copy.start()
        started.append(copy)
        return copy

    def lanes(half):
        return pl.ds(pl.multiple_of(half * W, 128), W)

    def rows(span):
        return pl.ds(span[0], span[1])

    def length_of(n, q, way):
        return n // 2 - (q + way) % 2

    def gather(view, to, n):
        flows = {}

        def start(q):
            for way, sign in ((0, 1), (1, -1)):
                flows[way, q, 1] = message(view(0, q), view(0, q), to(sign))

        def advance(step, q):
            for way, sign in ((0, 1), (1, -1)):
                length = length_of(n, q, way)
                if step <= length:
                    flows[way, q, step].wait_recv()
                if step < length:
                    block = view(-sign * step, q)
                    flows[way, q, step + 1] = message(block, block, to(sign))

        return start, advance

    def reduce(name, piece, to, n, finish, count, last_to=None):
        flows = {}

        def buffer(kind, q, way, step):
            return getattr(s, f"{name}_{kind}{q}").at[way, step - 1]

        for step in range(1, n // 2 + 1):
            for q in range(count):
                for way, sign in ((0, 1), (1, -1)):
                    first = n // 2 + 1 - length_of(n, q, way)
                    if step < first:
                        continue
                    value = piece(q, sign * (n // 2 + 1 - step))
                    if step > first:
                        flows[way, q, step - 1].wait_recv()
                        value = value + buffer("r", q, way, step - 1)[...].astype(F32)
                    buffer("s", q, way, step)[...] = value.astype(BF16)
                    where = to(sign) if step < n // 2 or last_to is None else last_to(q, sign)
                    flows[way, q, step] = message(buffer("s", q, way, step), buffer("r", q, way, step), where)
            yield
        for q in range(count):
            total = None
            for way in (0, 1):
                flows[way, q, n // 2].wait_recv()
                value = buffer("r", q, way, n // 2)[...].astype(F32)
                total = value if total is None else total + value
            finish(q, total)
        yield

    barrier = pltpu.get_barrier_semaphore()
    peers = [at(x_at=xo(a), y_at=yo(b)) for a in range(4) for b in range(4) if a or b]
    peers += [to_z(o) for o in range(1, 8)]
    peers += [twin, at(x_at=xo(2), core_at=1 - core)] + [at(z_at=zo(o), x_at=xo(2)) for o in (1, -1)]
    loads = [
        pltpu.make_async_copy(src, dst, s.load_sem.at[k])
        for k, (src, dst) in enumerate(((th_any, s.th), (tf_any, s.tf), (xh_any, s.xh), (xf_any, s.xf)))
    ]
    for copy in loads:
        copy.start()
    for peer in peers:
        pl.semaphore_signal(barrier, inc=1, device_id=peer, device_id_type=MESH)

    def padded(value, count):
        return jnp.concatenate([value, jnp.zeros((count - value.shape[0],) + value.shape[1:], value.dtype)], axis=0)

    def send_sums(ref, value):
        wide = jnp.broadcast_to(jnp.sum(value, axis=1, keepdims=True), (RT, 128))
        ref[mp] = padded(wide, 256).T[0:8]

        def send():
            return [
                message(ref.at[mp], ref.at[mp], where)
                for where in (twin, to_x(2), at(x_at=xo(2), core_at=1 - core))
            ]

        return send

    def sums_of(ref, got):
        for copy in got:
            copy.wait_recv()
        total = (ref[0] + ref[1]) + (ref[2] + ref[3])
        return jnp.broadcast_to(total[0:1], (128, 256)).T[0:RT]

    loads[0].wait()
    loads[1].wait()
    txt_pre = padded(jnp.dot(s.tf[...], s.th[...], preferred_element_type=F32), RT)
    s.dir_t[...] = txt_pre
    send_t = send_sums(s.sums_t, txt_pre * txt_pre)
    pl.semaphore_wait(barrier, len(peers))
    sent_t = send_t()
    loads[2].wait()
    loads[3].wait()
    img_pre = padded(jnp.dot(s.xf[...], s.xh[...], preferred_element_type=F32), RT)
    s.dir_i[...] = img_pre
    sent_i = send_sums(s.sums_i, img_pre * img_pre)()
    norm = jnp.sqrt(sums_of(s.sums_t, sent_t) + 1e-06)
    s.norm_t[...] = norm
    txt_dir = s.dir_t[...] / norm[:, 0:1]
    s.dir_t[...] = txt_dir

    own = lanes(xh)
    kinds = (own, lanes(1 - xh))
    s.texts_a[xl, y, :, own] = txt_dir[0:RA].astype(BF16)
    s.texts_b[xl, y, :, own] = txt_dir[RA:RT].astype(BF16)
    view = s.texts_a.at[xl, y, :, own]
    go_a1 = [message(view, view, to_x(o)) for o in (1, 2, 3)]
    view = s.texts_b.at[xl, y, :, own]
    go_b1 = [message(view, view, to_y(o)) for o in (1, 2, 3)]
    norm = jnp.sqrt(sums_of(s.sums_i, sent_i) + 1e-06)
    s.norm_i[...] = norm
    img_dir = s.dir_i[...] / norm[:, 0:1]
    s.dir_i[...] = img_dir
    s.parts[0] = padded(img_dir[0:64], RI).astype(BF16)
    s.parts[1] = img_dir[64:144].astype(BF16)
    swap = message(s.parts.at[1 - xh], s.images.at[z, :, own], to_x(2))
    s.images[z, :, own] = s.parts[xh]

    def image_chunk(o, q):
        kind, span = I_CHUNKS[q]
        return s.images.at[zo(o), rows(span), kinds[kind]]

    start, advance = gather(image_chunk, to_z, 8)
    start(0)
    start(1)
    swap.wait_recv()
    start(2)
    start(3)
    advance(1, 0)
    advance(1, 1)
    for copy in go_a1:
        copy.wait_recv()
    view = s.texts_a.at[:, y]
    go_a2 = [message(view, view, to_y(o)) for o in (1, 2, 3)]
    for copy in go_b1:
        copy.wait_recv()
    view = s.texts_b.at[xl, :, :, own]
    go_b2 = [message(view, view, to_x(o)) for o in (1, 2, 3)]
    advance(1, 2)
    advance(1, 3)
    for step in (2, 3, 4):
        for q in range(4):
            advance(step, q)

    temper = jnp.exp(jnp.full((1, 128), log_temp[0], F32))[:, 0:1]
    bias = logit_bias[0]
    half = pl.ds(core * 4, 4)

    def products(part, count):
        texts, theirs, got, mine = (getattr(s, f"{k}_{part}") for k in ("texts", "theirs", "got", "mine"))
        columns = texts[...].reshape(8 * count, 2 * W)
        theirs[...] = lax.dot_general(
            s.images[pl.ds((1 - core) * 4, 4)].reshape(4 * RI, 2 * W), columns, NT, preferred_element_type=F32
        ).reshape(4, RI, 8 * count)
        cross = message(theirs, got, twin)
        mine[...] = lax.dot_general(
            s.images[half].reshape(4 * RI, 2 * W), columns, NT, preferred_element_type=F32
        ).reshape(4, RI, 8 * count)
        return cross

    def pairs(part, count, first, cross):
        got, mine, pg = (getattr(s, f"{k}_{part}") for k in ("got", "mine", "pg"))
        shape = (RI, 8 * count)
        ahead = lax.broadcasted_iota(jnp.int32, shape, 1) - lax.broadcasted_iota(jnp.int32, shape, 0)
        column = lax.broadcasted_iota(jnp.int32, (1, 8 * count), 1) - slot * count
        here = (column >= 0) & (column < count)
        cross.wait_recv()

        @pl.loop(0, 4)
        def _(block):
            logits = temper * (mine[block] + got[block]) + bias
            same = here & (ahead == jnp.where(core * 4 + block == z, slot * count + 64 * xh - first, -8192))
            pg[core * 4 + block] = (temper * (jax.nn.sigmoid(logits) - same.astype(F32))).astype(BF16)

        return message(pg.at[half], pg.at[half], twin)

    def text_grads(part, count):
        pg, grad, grad_s = (getattr(s, k) for k in (f"pg_{part}", f"grad_{part}", f"grad_{part}s"))
        value = lax.dot_general(
            pg[...].reshape(8 * RI, 8 * count), s.images[...].reshape(8 * RI, 2 * W), TN, preferred_element_type=F32
        ).reshape(2, 4, count, 2 * W)
        grad[...] = value
        grad_s[...] = value.astype(BF16)

    for copy in go_a2:
        copy.wait_recv()
    cross_a = products("a", RA)
    share_a = pairs("a", RA, 0, cross_a)
    for copy in go_b2:
        copy.wait_recv()
    cross_b = products("b", RB)
    share_a.wait_recv()
    text_grads("a", RA)
    back_a1 = [message(s.grad_as.at[:, yo(o)], s.a1.at[o - 1], to_y(o)) for o in (1, 2, 3)]
    share_b = pairs("b", RB, RA, cross_b)
    s.grad_i[...] = lax.dot_general(
        s.pg_a[...].reshape(8 * RI, 8 * RA), s.texts_a[...].reshape(8 * RA, 2 * W), NN, preferred_element_type=F32
    ).reshape(8, RI, 2 * W)
    share_b.wait_recv()
    text_grads("b", RB)
    back_b1 = [
        message(s.grad_bs.at[lax.rem(xo(o), 2), :, :, lanes(lax.div(xo(o), 2))], s.b1.at[o - 1], to_x(o))
        for o in (1, 2, 3)
    ]
    s.grad_i[...] += lax.dot_general(
        s.pg_b[...].reshape(8 * RI, 8 * RB), s.texts_b[...].reshape(8 * RB, 2 * W), NN, preferred_element_type=F32
    ).reshape(8, RI, 2 * W)

    def image_term(q, o):
        kind, span = I_CHUNKS[q]
        return s.grad_i[zo(o), rows(span), kinds[kind]]

    def image_done(q, total):
        kind, span = I_CHUNKS[q]
        if kind == 0:
            s.both[xh, rows(span)] = total + image_term(q, 0)
        else:
            s.both[1 - xh, rows(span)] = total

    back_z = reduce(
        "img", image_term, to_z, 8, image_done, 4,
        lambda q, sign: to_z(sign) if I_CHUNKS[q][0] == 0 else at(z_at=zo(sign), x_at=xo(2)),
    )
    next(back_z)
    s.swap_s[...] = s.grad_i[z, :, kinds[1]].astype(BF16)
    swap_back = message(s.swap_s, s.swap_r, to_x(2))
    next(back_z)
    next(back_z)
    for copy in back_a1:
        copy.wait_recv()
    s.a_sum[...] = s.grad_a[:, y] + sum(s.a1[o].astype(F32) for o in range(3))
    s.a_s[...] = s.a_sum[...].astype(BF16)
    back_a2 = [
        message(s.a_s.at[lax.rem(xo(o), 2), :, lanes(lax.div(xo(o), 2))], s.a2.at[o - 1], to_x(o)) for o in (1, 2, 3)
    ]
    next(back_z)
    for copy in back_b1:
        copy.wait_recv()
    s.b_sum[...] = s.grad_b[xl, :, :, own] + sum(s.b1[o].astype(F32) for o in range(3))
    s.b_s[...] = s.b_sum[...].astype(BF16)
    back_b2 = [message(s.b_s.at[yo(o)], s.b2.at[o - 1], to_y(o)) for o in (1, 2, 3)]
    next(back_z)
    swap_back.wait_recv()
    s.both[1 - xh] += s.swap_r[...].astype(F32)
    img_unit_grad = jnp.concatenate([s.both[0, pl.ds(0, 64)], s.both[1]], axis=0)
    sent_i = send_sums(s.along_i, img_unit_grad * s.dir_i[...])()
    for copy in back_a2:
        copy.wait_recv()
    s.t_sum[pl.ds(0, RA)] = s.a_sum[xl, :, own] + sum(s.a2[o].astype(F32) for o in range(3))
    for copy in back_b2:
        copy.wait_recv()
    s.t_sum[pl.ds(RA, RB)] = s.b_sum[y] + sum(s.b2[o].astype(F32) for o in range(3))
    sent_t = send_sums(s.along_t, s.t_sum[...] * s.dir_t[...])()

    along = sums_of(s.along_i, sent_i)
    img_unit_grad = jnp.concatenate([s.both[0, pl.ds(0, 64)], s.both[1]], axis=0)
    img_grad = ((img_unit_grad - s.dir_i[...] * along[:, 0:1]) / s.norm_i[:, 0:1]).astype(BF16)
    s.head_i[...] = lax.dot_general(s.xf[...], img_grad[0:R], TN, preferred_element_type=F32)
    for j in range(8):
        s.si[j] = jnp.concatenate([s.head_i[pl.ds(k * 192 + j * 24, 24), :] for k in range(8)], axis=0).astype(BF16)

    def over_xy(src, dst):
        copies = []
        for a in (1, 0):
            for b in (2, 1, 3, 0):
                if a or b:
                    to_xl = lax.rem(xl + a, 2)
                    where = at(x_at=xh * 2 + to_xl, y_at=yo(b))
                    copies.append(message(src.at[to_xl * 4 + yo(b)], dst.at[a * 4 + b - 1], where))
        return copies

    fore_i = over_xy(s.si, s.ri)
    along = sums_of(s.along_t, sent_t)
    txt_grad = ((s.t_sum[...] - s.dir_t[...] * along[:, 0:1]) / s.norm_t[:, 0:1]).astype(BF16)
    s.head_t[...] = lax.dot_general(s.tf[...], txt_grad[0:R], TN, preferred_element_type=F32)

    def text_term(q, o):
        return s.head_t[pl.ds(pl.multiple_of(zo(o) * RT + T_CHUNKS[q][0], 16), T_CHUNKS[q][1]), :]

    def text_done(q, total):
        s.t_sum[rows(T_CHUNKS[q])] = total + text_term(q, 0)

    fore_t = reduce("ht", text_term, to_z, 8, text_done, 4)
    next(fore_t)
    next(fore_t)
    next(fore_t)
    next(fore_t)
    for copy in fore_i:
        copy.wait_recv()
    for k in range(8):
        s.zi[k] = s.head_i[pl.ds(pl.multiple_of(k * 192 + slot * 24, 8), 24), :]
    s.zi[...] += sum(s.ri[j].astype(F32) for j in range(7)).reshape(8, 24, W)
    for k in range(8):
        s.zi_s[k] = padded(s.zi[k], 32).astype(BF16)
    last_i = [message(s.zi_s.at[zo(o)], s.zi_r.at[o - 1], to_z(o)) for o in (4, 3, 5, 2, 6, 1, 7)]
    next(fore_t)
    total = s.t_sum[...]
    for j in range(8):
        s.xt[j] = padded(total[18 * j : 18 * j + 18], 24)
    last_t = over_xy(s.xt, s.xt_r)
    for copy in last_t:
        copy.wait_recv()
    out_t[...] = (s.xt[slot] + sum(s.xt_r[j] for j in range(7)))[0:18]
    for copy in last_i:
        copy.wait_recv()
    out_i[...] = s.zi[z] + sum(s.zi_r[j].astype(F32) for j in range(7))[0:24]
    for copy in started:
        copy.wait_send()


def body(image_feats, text_feats, image_head, text_head, log_temp, logit_bias):
    vmem = pl.BlockSpec(memory_space=pltpu.VMEM)
    smem = pl.BlockSpec(memory_space=pltpu.SMEM)
    anywhere = pl.BlockSpec(memory_space=pl.ANY)
    scratch = scratch_of()

    def run(*refs):
        kernel(tuple(scratch), *refs)

    return pl.pallas_call(
        run,
        out_shape=(jax.ShapeDtypeStruct((24, W), F32), jax.ShapeDtypeStruct((18, W), F32)),
        in_specs=[anywhere, anywhere, anywhere, anywhere, smem, smem],
        out_specs=(vmem, vmem),
        scratch_shapes=list(scratch.values()),
        compiler_params=pltpu.CompilerParams(
            collective_id=0, has_side_effects=True, vmem_limit_bytes=56 * 1024 * 1024
        ),
        name="pair_loss",
    )(image_feats, text_feats, image_head, text_head, log_temp, logit_bias)


def solution(mesh):
    placed = (P("dp", None), P("dp", None), P(None, "mp"), P(None, "mp"), P(), P())
    return jax.shard_map(
        body, mesh=mesh, in_specs=placed, out_specs=(P("dp", "mp"), P("dp", "mp")), check_vma=False
    )
```

time: 1440 us -> 97.8 us (0.07)
  the two profiles are of different devices: /device:TPU:4 before, /device:TPU:1 now
where the time goes in v2:
time: 97.8 us; the launch traced here: 97.6 us
  Pallas kernels  92.8 us (95%)
  local copies, waits for them, and re-layouts  2.77 us (3%)
  between operations  1.93 us (2%)
    pallas_call x1, Pallas kernels, body(): pl.pallas_call(run, out_shape=(jax.ShapeDtypeStruct((24, W), F32), jax.Sh...  92.8 us
    unnamed x2, local copies, waits for them, and re-layouts  2.77 us

profile of v2, /device:TPU:1, one launch (start us, length us, event | category | flops | bytes accessed | tf_op | source)
XLA Modules:
  0.0 97.6 jit_solution(445063170207309220)
XLA Ops:
  1.9 92.8 %pair_loss.1 = (f32[24,384]{1,0:T(8,128)}, f32[18,384]{1,0:T(8,128)}) custom-call(bf16[136,1536]{1,0:T(8,128)(2,1)} %refs_0_.1, bf16[136,1152]{1,0:T(8,128)(2,1)} %refs_1_.1, bf16[1536,384]{1,0:T(8,128)(2,1)} %refs_2_.1, bf16[1152,384]{1,0:T(8,128)(2,1)} %refs_3_.1, f32[1]{0:T(128)S(6)} %copy.10.refs_4_, f32[1]{0:T(128)S(6)} %copy.11.refs_5_), custom_call_target="tpu_custom_call" | custom-call | tf_op jit(solution)/shard_map/pair_loss/pallas_call | solution.py:442
  94.8 1.4 %copy.12 = f32[24,384]{1,0:T(8,128)} copy(f32[24,384]{1,0:T(8,128)} %get-tuple-element.4) | data formatting | bytes 73728
  96.2 1.4 %copy.13 = f32[18,384]{1,0:T(8,128)} copy(f32[18,384]{1,0:T(8,128)} %get-tuple-element.5) | data formatting | bytes 55296

commit v3 on v2

--- a/solution.py
+++ b/solution.py
@@ -34,6 +34,8 @@
 def scratch_of():
     made = dict(
         xf=bf16(R, 1536), tf=bf16(R, 1152), xh=bf16(1536, W), th=bf16(1152, W),
+        texts_an=bf16(2, 4, RA, 2 * W), texts_bn=bf16(2, 4, RB, 2 * W), images_n=bf16(8, RI, 2 * W),
+        all_t=f32(8, 8, 256), all_i=f32(8, 8, 256), columns_t=f32(256, 128), columns_i=f32(256, 128),
         sums_t=f32(4, 8, 256), sums_i=f32(4, 8, 256), along_t=f32(4, 8, 256), along_i=f32(4, 8, 256),
         norm_t=f32(RT, 128), norm_i=f32(RT, 128), dir_t=f32(RT, W), dir_i=f32(RT, W),
         parts=bf16(2, RI, W), texts_a=bf16(2, 4, RA, 2 * W), texts_b=bf16(2, 4, RB, 2 * W), images=bf16(8, RI, 2 * W),
@@ -113,6 +115,13 @@
         copy.start()
         started.append(copy)
         return copy
+
+    flushed = [0]
+
+    def flush(upto):
+        for copy in started[flushed[0] : upto]:
+            copy.wait_send()
+        flushed[0] = max(upto, flushed[0])
 
     def lanes(half):
         return pl.ds(pl.multiple_of(half * W, 128), W)
@@ -201,40 +210,46 @@
     def sums_of(ref, got):
         for copy in got:
             copy.wait_recv()
-        total = (ref[0] + ref[1]) + (ref[2] + ref[3])
+        return (ref[0] + ref[1]) + (ref[2] + ref[3])
+
+    def down(total):
         return jnp.broadcast_to(total[0:1], (128, 256)).T[0:RT]
+
+    def over_xy(src, dst, place=None):
+        copies = []
+        for a in (1, 0):
+            for b in (2, 1, 3, 0):
+                if a or b:
+                    to_xl = lax.rem(xl + a, 2)
+                    where = at(x_at=xh * 2 + to_xl, y_at=yo(b))
+                    if place is None:
+                        copies.append(message(src.at[to_xl * 4 + yo(b)], dst.at[a * 4 + b - 1], where))
+                    else:
+                        copies.append(message(src.at[place], dst.at[place], where))
+        return copies
 
     loads[0].wait()
     loads[1].wait()
     txt_pre = padded(jnp.dot(s.tf[...], s.th[...], preferred_element_type=F32), RT)
     s.dir_t[...] = txt_pre
     send_t = send_sums(s.sums_t, txt_pre * txt_pre)
+    own = lanes(xh)
+    kinds = (own, lanes(1 - xh))
+    s.texts_a[xl, y, :, own] = txt_pre[0:RA].astype(BF16)
+    s.texts_b[xl, y, :, own] = txt_pre[RA:RT].astype(BF16)
     pl.semaphore_wait(barrier, len(peers))
+
     sent_t = send_t()
+    view = s.texts_a.at[xl, y, :, own]
+    go_a1 = [message(view, view, to_x(o)) for o in (1, 2, 3)]
+    view = s.texts_b.at[xl, y, :, own]
+    go_b1 = [message(view, view, to_y(o)) for o in (1, 2, 3)]
     loads[2].wait()
     loads[3].wait()
     img_pre = padded(jnp.dot(s.xf[...], s.xh[...], preferred_element_type=F32), RT)
     s.dir_i[...] = img_pre
-    sent_i = send_sums(s.sums_i, img_pre * img_pre)()
-    norm = jnp.sqrt(sums_of(s.sums_t, sent_t) + 1e-06)
-    s.norm_t[...] = norm
-    txt_dir = s.dir_t[...] / norm[:, 0:1]
-    s.dir_t[...] = txt_dir
-
-    own = lanes(xh)
-    kinds = (own, lanes(1 - xh))
-    s.texts_a[xl, y, :, own] = txt_dir[0:RA].astype(BF16)
-    s.texts_b[xl, y, :, own] = txt_dir[RA:RT].astype(BF16)
-    view = s.texts_a.at[xl, y, :, own]
-    go_a1 = [message(view, view, to_x(o)) for o in (1, 2, 3)]
-    view = s.texts_b.at[xl, y, :, own]
-    go_b1 = [message(view, view, to_y(o)) for o in (1, 2, 3)]
-    norm = jnp.sqrt(sums_of(s.sums_i, sent_i) + 1e-06)
-    s.norm_i[...] = norm
-    img_dir = s.dir_i[...] / norm[:, 0:1]
-    s.dir_i[...] = img_dir
-    s.parts[0] = padded(img_dir[0:64], RI).astype(BF16)
-    s.parts[1] = img_dir[64:144].astype(BF16)
+    s.parts[0] = padded(img_pre[0:64], RI).astype(BF16)
+    s.parts[1] = img_pre[64:144].astype(BF16)
     swap = message(s.parts.at[1 - xh], s.images.at[z, :, own], to_x(2))
     s.images[z, :, own] = s.parts[xh]
 
@@ -245,6 +260,9 @@
     start, advance = gather(image_chunk, to_z, 8)
     start(0)
     start(1)
+    sent_i = send_sums(s.sums_i, img_pre * img_pre)()
+    s.all_t[slot] = sums_of(s.sums_t, sent_t)
+    norms_t = over_xy(s.all_t, s.all_t, slot)
     swap.wait_recv()
     start(2)
     start(3)
@@ -258,25 +276,58 @@
         copy.wait_recv()
     view = s.texts_b.at[xl, :, :, own]
     go_b2 = [message(view, view, to_x(o)) for o in (1, 2, 3)]
+    s.all_i[z] = sums_of(s.sums_i, sent_i)
+    norms_i = [message(s.all_i.at[z], s.all_i.at[z], to_z(o)) for o in range(1, 8)]
     advance(1, 2)
     advance(1, 3)
-    for step in (2, 3, 4):
-        for q in range(4):
-            advance(step, q)
+    for name, place in (("t", slot), ("i", z)):
+        norm = jnp.sqrt(down(getattr(s, f"all_{name}")[place]) + 1e-06)
+        getattr(s, f"norm_{name}")[...] = norm
+        side = getattr(s, f"dir_{name}")
+        side[...] = side[...] / norm[:, 0:1]
+    for q in range(4):
+        advance(2, q)
+
+    def columns_of(name, copies):
+        for copy in copies:
+            copy.wait_recv()
+        every = getattr(s, f"all_{name}")
+        sums = jnp.concatenate([every[k, 0:1] for k in range(8)], axis=0)
+        getattr(s, f"columns_{name}")[...] = padded(1.0 / jnp.sqrt(sums + 1e-06), 128).T
+
+    columns_of("t", norms_t)
+    for q in range(4):
+        advance(3, q)
+    columns_of("i", norms_i)
+    for q in range(4):
+        advance(4, q)
+    for k in range(8):
+        s.images_n[k] = (s.images[k].astype(F32) * s.columns_i[pl.ds(pl.multiple_of(xh * 64, 8), RI), k : k + 1]).astype(BF16)
+
+    def text_units(part, first, count, copies):
+        for copy in copies:
+            copy.wait_recv()
+        texts, units = getattr(s, f"texts_{part}"), getattr(s, f"texts_{part}n")
+        for k in range(8):
+            units[k // 4, k % 4] = (
+                texts[k // 4, k % 4].astype(F32) * s.columns_t[pl.ds(first, count), k : k + 1]
+            ).astype(BF16)
 
     temper = jnp.exp(jnp.full((1, 128), log_temp[0], F32))[:, 0:1]
     bias = logit_bias[0]
     half = pl.ds(core * 4, 4)
 
     def products(part, count):
-        texts, theirs, got, mine = (getattr(s, f"{k}_{part}") for k in ("texts", "theirs", "got", "mine"))
+        texts, theirs, got, mine = (
+            getattr(s, k) for k in (f"texts_{part}n", f"theirs_{part}", f"got_{part}", f"mine_{part}")
+        )
         columns = texts[...].reshape(8 * count, 2 * W)
         theirs[...] = lax.dot_general(
-            s.images[pl.ds((1 - core) * 4, 4)].reshape(4 * RI, 2 * W), columns, NT, preferred_element_type=F32
+            s.images_n[pl.ds((1 - core) * 4, 4)].reshape(4 * RI, 2 * W), columns, NT, preferred_element_type=F32
         ).reshape(4, RI, 8 * count)
         cross = message(theirs, got, twin)
         mine[...] = lax.dot_general(
-            s.images[half].reshape(4 * RI, 2 * W), columns, NT, preferred_element_type=F32
+            s.images_n[half].reshape(4 * RI, 2 * W), columns, NT, preferred_element_type=F32
         ).reshape(4, RI, 8 * count)
         return cross
 
@@ -299,24 +350,23 @@
     def text_grads(part, count):
         pg, grad, grad_s = (getattr(s, k) for k in (f"pg_{part}", f"grad_{part}", f"grad_{part}s"))
         value = lax.dot_general(
-            pg[...].reshape(8 * RI, 8 * count), s.images[...].reshape(8 * RI, 2 * W), TN, preferred_element_type=F32
+            pg[...].reshape(8 * RI, 8 * count), s.images_n[...].reshape(8 * RI, 2 * W), TN, preferred_element_type=F32
         ).reshape(2, 4, count, 2 * W)
         grad[...] = value
         grad_s[...] = value.astype(BF16)
 
-    for copy in go_a2:
-        copy.wait_recv()
+    text_units("a", 0, RA, go_a2)
     cross_a = products("a", RA)
     share_a = pairs("a", RA, 0, cross_a)
-    for copy in go_b2:
-        copy.wait_recv()
+    text_units("b", RA, RB, go_b2)
+    arrived = len(started)
     cross_b = products("b", RB)
     share_a.wait_recv()
     text_grads("a", RA)
     back_a1 = [message(s.grad_as.at[:, yo(o)], s.a1.at[o - 1], to_y(o)) for o in (1, 2, 3)]
     share_b = pairs("b", RB, RA, cross_b)
     s.grad_i[...] = lax.dot_general(
-        s.pg_a[...].reshape(8 * RI, 8 * RA), s.texts_a[...].reshape(8 * RA, 2 * W), NN, preferred_element_type=F32
+        s.pg_a[...].reshape(8 * RI, 8 * RA), s.texts_an[...].reshape(8 * RA, 2 * W), NN, preferred_element_type=F32
     ).reshape(8, RI, 2 * W)
     share_b.wait_recv()
     text_grads("b", RB)
@@ -325,7 +375,7 @@
         for o in (1, 2, 3)
     ]
     s.grad_i[...] += lax.dot_general(
-        s.pg_b[...].reshape(8 * RI, 8 * RB), s.texts_b[...].reshape(8 * RB, 2 * W), NN, preferred_element_type=F32
+        s.pg_b[...].reshape(8 * RI, 8 * RB), s.texts_bn[...].reshape(8 * RB, 2 * W), NN, preferred_element_type=F32
     ).reshape(8, RI, 2 * W)
 
     def image_term(q, o):
@@ -346,6 +396,7 @@
     next(back_z)
     s.swap_s[...] = s.grad_i[z, :, kinds[1]].astype(BF16)
     swap_back = message(s.swap_s, s.swap_r, to_x(2))
+    flush(arrived)
     next(back_z)
     next(back_z)
     for copy in back_a1:
@@ -365,6 +416,7 @@
     swap_back.wait_recv()
     s.both[1 - xh] += s.swap_r[...].astype(F32)
     img_unit_grad = jnp.concatenate([s.both[0, pl.ds(0, 64)], s.both[1]], axis=0)
+    returned = len(started)
     sent_i = send_sums(s.along_i, img_unit_grad * s.dir_i[...])()
     for copy in back_a2:
         copy.wait_recv()
@@ -374,25 +426,15 @@
     s.t_sum[pl.ds(RA, RB)] = s.b_sum[y] + sum(s.b2[o].astype(F32) for o in range(3))
     sent_t = send_sums(s.along_t, s.t_sum[...] * s.dir_t[...])()
 
-    along = sums_of(s.along_i, sent_i)
+    along = down(sums_of(s.along_i, sent_i))
     img_unit_grad = jnp.concatenate([s.both[0, pl.ds(0, 64)], s.both[1]], axis=0)
     img_grad = ((img_unit_grad - s.dir_i[...] * along[:, 0:1]) / s.norm_i[:, 0:1]).astype(BF16)
     s.head_i[...] = lax.dot_general(s.xf[...], img_grad[0:R], TN, preferred_element_type=F32)
     for j in range(8):
         s.si[j] = jnp.concatenate([s.head_i[pl.ds(k * 192 + j * 24, 24), :] for k in range(8)], axis=0).astype(BF16)
 
-    def over_xy(src, dst):
-        copies = []
-        for a in (1, 0):
-            for b in (2, 1, 3, 0):
-                if a or b:
-                    to_xl = lax.rem(xl + a, 2)
-                    where = at(x_at=xh * 2 + to_xl, y_at=yo(b))
-                    copies.append(message(src.at[to_xl * 4 + yo(b)], dst.at[a * 4 + b - 1], where))
-        return copies
-
     fore_i = over_xy(s.si, s.ri)
-    along = sums_of(s.along_t, sent_t)
+    along = down(sums_of(s.along_t, sent_t))
     txt_grad = ((s.t_sum[...] - s.dir_t[...] * along[:, 0:1]) / s.norm_t[:, 0:1]).astype(BF16)
     s.head_t[...] = lax.dot_general(s.tf[...], txt_grad[0:R], TN, preferred_element_type=F32)
 
@@ -404,6 +446,7 @@
 
     fore_t = reduce("ht", text_term, to_z, 8, text_done, 4)
     next(fore_t)
+    flush(returned)
     next(fore_t)
     next(fore_t)
     next(fore_t)
@@ -419,15 +462,16 @@
     total = s.t_sum[...]
     for j in range(8):
         s.xt[j] = padded(total[18 * j : 18 * j + 18], 24)
+    before = len(started)
     last_t = over_xy(s.xt, s.xt_r)
+    flush(before)
     for copy in last_t:
         copy.wait_recv()
     out_t[...] = (s.xt[slot] + sum(s.xt_r[j] for j in range(7)))[0:18]
     for copy in last_i:
         copy.wait_recv()
     out_i[...] = s.zi[z] + sum(s.zi_r[j].astype(F32) for j in range(7))[0:24]
-    for copy in started:
-        copy.wait_send()
+    flush(len(started))
 
 
 def body(image_feats, text_feats, image_head, text_head, log_temp, logit_bias):
@@ -439,7 +483,7 @@
     def run(*refs):
         kernel(tuple(scratch), *refs)
 
-    return pl.pallas_call(
+    found = pl.pallas_call(
         run,
         out_shape=(jax.ShapeDtypeStruct((24, W), F32), jax.ShapeDtypeStruct((18, W), F32)),
         in_specs=[anywhere, anywhere, anywhere, anywhere, smem, smem],
@@ -451,6 +495,18 @@
         name="pair_loss",
     )(image_feats, text_feats, image_head, text_head, log_temp, logit_bias)
 
+    def hand_over(a, b, c, d):
+        c[...] = a[...]
+        d[...] = b[...]
+
+    return pl.pallas_call(
+        hand_over,
+        out_shape=(jax.ShapeDtypeStruct((24, W), F32), jax.ShapeDtypeStruct((18, W), F32)),
+        in_specs=[vmem, vmem],
+        out_specs=(vmem, vmem),
+        name="hand_over",
+    )(*found)
+
 
 def solution(mesh):
     placed = (P("dp", None), P("dp", None), P(None, "mp"), P(None, "mp"), P(), P())

time: 97.8 us -> 93.7 us (0.958)
  local copies, waits for them, and re-layouts: 2.77 us -> 0 us
  Pallas kernels: 92.8 us -> 91.6 us
    unnamed x2 -> x0, local copies, waits for them, and re-layouts: 2.77 us -> none
    pallas_call x1, Pallas kernels: 92.8 us -> 90.1 us  [body(): pl.pallas_call(run, out_shape=(jax.ShapeDtypeStruct((24, W), F32), jax.Sh...]
    pallas_call x0 -> x1, Pallas kernels: none -> 1.42 us  [body(): pl.pallas_call(hand_over, out_shape=(jax.ShapeDtypeStruct((24, W), F32),...]
where the time goes in v3:
time: 93.7 us; the launch traced here: 93.5 us
  Pallas kernels  91.6 us (98%)
  between operations  1.93 us (2%)
    pallas_call x1, Pallas kernels, body(): pl.pallas_call(run, out_shape=(jax.ShapeDtypeStruct((24, W), F32), jax.Sh...  90.1 us

profile of v3, /device:TPU:1, one launch (start us, length us, event | category | flops | bytes accessed | tf_op | source)
XLA Modules:
  0.0 93.5 jit_solution(7618348562684830988)
XLA Ops:
  1.9 90.1 %pair_loss.1 = (f32[24,384]{1,0:T(8,128)}, f32[18,384]{1,0:T(8,128)}) custom-call(bf16[136,1536]{1,0:T(8,128)(2,1)} %refs_0_.1, bf16[136,1152]{1,0:T(8,128)(2,1)} %refs_1_.1, bf16[1536,384]{1,0:T(8,128)(2,1)} %refs_2_.1, bf16[1152,384]{1,0:T(8,128)(2,1)} %refs_3_.1, f32[1]{0:T(128)S(6)} %copy.8.refs_4_, f32[1]{0:T(128)S(6)} %copy.9.refs_5_), custom_call_target="tpu_custom_call" | custom-call | tf_op jit(solution)/shard_map/pair_loss/pallas_call | solution.py:486
  92.1 1.4 %hand_over.1 = (f32[24,384]{1,0:T(8,128)}, f32[18,384]{1,0:T(8,128)}) custom-call(f32[24,384]{1,0:T(8,128)} %get-tuple-element.4.a, f32[18,384]{1,0:T(8,128)} %get-tuple-element.5.b), custom_call_target="tpu_custom_call" | custom-call | tf_op jit(solution)/shard_map/hand_over/pallas_call | solution.py:502

commit v4 on v3

--- a/solution.py
+++ b/solution.py
@@ -18,7 +18,7 @@
 RI = 80
 W = 384
 MESSAGES = 200
-RA, RB = 64, 80
+RA, RB = 80, 64
 I_CHUNKS = ((0, (0, 48)), (0, (48, 32)), (1, (0, 48)), (1, (48, 32)))
 T_CHUNKS = ((0, 32), (32, 32), (64, 32), (96, 48))
 
@@ -46,8 +46,8 @@
         a1=bf16(3, 2, RA, 2 * W), a_sum=f32(2, RA, 2 * W), a_s=bf16(2, RA, 2 * W), a2=bf16(3, RA, W),
         b1=bf16(3, 4, RB, W), b_sum=f32(4, RB, W), b_s=bf16(4, RB, W), b2=bf16(3, RB, W),
         swap_s=bf16(RI, W), swap_r=bf16(RI, W), both=f32(2, RI, W), t_sum=f32(RT, W),
-        head_t=f32(1152, W), head_i=f32(1536, W), si=bf16(8, 192, W), ri=bf16(7, 192, W),
-        zi=f32(8, 24, W), zi_s=bf16(8, 32, W), zi_r=bf16(7, 32, W), xt=f32(8, 24, W), xt_r=f32(7, 24, W),
+        head_t=f32(1152, W), head_i=f32(1536, W), si0=bf16(8, 192, 256), ri0=bf16(7, 192, 256), si1=bf16(8, 192, 128), ri1=bf16(7, 192, 128),
+        zi=f32(8, 24, W), zi_s0=bf16(8, 32, 256), zi_r0=bf16(7, 32, 256), zi_s1=bf16(8, 32, 128), zi_r1=bf16(7, 32, 128), xt=f32(8, 24, W), xt_r=f32(7, 24, W),
     )
 
     def ring(name, steps, *shapes):
@@ -60,7 +60,8 @@
     made.update(
         send_sem=pltpu.SemaphoreType.DMA((MESSAGES,)),
         recv_sem=pltpu.SemaphoreType.DMA((MESSAGES,)),
-        load_sem=pltpu.SemaphoreType.DMA((4,)),
+        load_sem=pltpu.SemaphoreType.DMA((6,)),
+        scale=pltpu.SMEM((1,), F32), bias=pltpu.SMEM((1,), F32),
     )
     return made
 
@@ -185,7 +186,9 @@
     peers += [twin, at(x_at=xo(2), core_at=1 - core)] + [at(z_at=zo(o), x_at=xo(2)) for o in (1, -1)]
     loads = [
         pltpu.make_async_copy(src, dst, s.load_sem.at[k])
-        for k, (src, dst) in enumerate(((th_any, s.th), (tf_any, s.tf), (xh_any, s.xh), (xf_any, s.xf)))
+        for k, (src, dst) in enumerate((
+            (th_any, s.th), (tf_any, s.tf), (xh_any, s.xh), (xf_any, s.xf), (log_temp, s.scale), (logit_bias, s.bias)
+        ))
     ]
     for copy in loads:
         copy.start()
@@ -292,17 +295,23 @@
         for copy in copies:
             copy.wait_recv()
         every = getattr(s, f"all_{name}")
-        sums = jnp.concatenate([every[k, 0:1] for k in range(8)], axis=0)
+        sums = jnp.concatenate([every[k if name == "t" else zo(k), 0:1] for k in range(8)], axis=0)
         getattr(s, f"columns_{name}")[...] = padded(1.0 / jnp.sqrt(sums + 1e-06), 128).T
 
+    def image_units(*distances):
+        for o in distances:
+            scale = s.columns_i[pl.ds(pl.multiple_of(xh * 64, 8), RI), o % 8 : o % 8 + 1]
+            s.images_n[zo(o)] = (s.images[zo(o)].astype(F32) * scale).astype(BF16)
+
     columns_of("t", norms_t)
+    columns_of("i", norms_i)
+    image_units(0, 1, -1)
     for q in range(4):
         advance(3, q)
-    columns_of("i", norms_i)
+    image_units(2, -2, 3, -3)
     for q in range(4):
         advance(4, q)
-    for k in range(8):
-        s.images_n[k] = (s.images[k].astype(F32) * s.columns_i[pl.ds(pl.multiple_of(xh * 64, 8), RI), k : k + 1]).astype(BF16)
+    image_units(4)
 
     def text_units(part, first, count, copies):
         for copy in copies:
@@ -313,8 +322,10 @@
                 texts[k // 4, k % 4].astype(F32) * s.columns_t[pl.ds(first, count), k : k + 1]
             ).astype(BF16)
 
-    temper = jnp.exp(jnp.full((1, 128), log_temp[0], F32))[:, 0:1]
-    bias = logit_bias[0]
+    loads[4].wait()
+    loads[5].wait()
+    temper = jnp.exp(jnp.full((1, 128), s.scale[0], F32))[:, 0:1]
+    bias = s.bias[0]
     half = pl.ds(core * 4, 4)
 
     def products(part, count):
@@ -430,10 +441,12 @@
     img_unit_grad = jnp.concatenate([s.both[0, pl.ds(0, 64)], s.both[1]], axis=0)
     img_grad = ((img_unit_grad - s.dir_i[...] * along[:, 0:1]) / s.norm_i[:, 0:1]).astype(BF16)
     s.head_i[...] = lax.dot_general(s.xf[...], img_grad[0:R], TN, preferred_element_type=F32)
-    for j in range(8):
-        s.si[j] = jnp.concatenate([s.head_i[pl.ds(k * 192 + j * 24, 24), :] for k in range(8)], axis=0).astype(BF16)
-
-    fore_i = over_xy(s.si, s.ri)
+    sides = ((pl.ds(0, 256), s.si0, s.ri0, s.zi_s0, s.zi_r0), (pl.ds(256, 128), s.si1, s.ri1, s.zi_s1, s.zi_r1))
+    for span, si, _, _, _ in sides:
+        for j in range(8):
+            si[j] = jnp.concatenate([s.head_i[pl.ds(k * 192 + j * 24, 24), span] for k in range(8)], axis=0).astype(BF16)
+
+    fore_i = [over_xy(si, ri) for _, si, ri, _, _ in sides]
     along = down(sums_of(s.along_t, sent_t))
     txt_grad = ((s.t_sum[...] - s.dir_t[...] * along[:, 0:1]) / s.norm_t[:, 0:1]).astype(BF16)
     s.head_t[...] = lax.dot_general(s.tf[...], txt_grad[0:R], TN, preferred_element_type=F32)
@@ -450,33 +463,37 @@
     next(fore_t)
     next(fore_t)
     next(fore_t)
-    for copy in fore_i:
-        copy.wait_recv()
-    for k in range(8):
-        s.zi[k] = s.head_i[pl.ds(pl.multiple_of(k * 192 + slot * 24, 8), 24), :]
-    s.zi[...] += sum(s.ri[j].astype(F32) for j in range(7)).reshape(8, 24, W)
-    for k in range(8):
-        s.zi_s[k] = padded(s.zi[k], 32).astype(BF16)
-    last_i = [message(s.zi_s.at[zo(o)], s.zi_r.at[o - 1], to_z(o)) for o in (4, 3, 5, 2, 6, 1, 7)]
-    next(fore_t)
-    total = s.t_sum[...]
-    for j in range(8):
-        s.xt[j] = padded(total[18 * j : 18 * j + 18], 24)
-    before = len(started)
-    last_t = over_xy(s.xt, s.xt_r)
+    last_i = []
+    for side, (span, _, ri, zi_s, zi_r) in enumerate(sides):
+        if side == 1:
+            next(fore_t)
+            before = len(started)
+            total = s.t_sum[...]
+            for j in range(8):
+                s.xt[j] = padded(total[18 * j : 18 * j + 18], 24)
+            last_t = over_xy(s.xt, s.xt_r)
+        for copy in fore_i[side]:
+            copy.wait_recv()
+        whole = sum(ri[j].astype(F32) for j in range(7))
+        for k in range(8):
+            s.zi[k, :, span] = (
+                s.head_i[pl.ds(pl.multiple_of(k * 192 + slot * 24, 8), 24), span] + whole[k * 24 : k * 24 + 24]
+            )
+            zi_s[k] = padded(s.zi[k, :, span], 32).astype(BF16)
+        last_i.append([message(zi_s.at[zo(o)], zi_r.at[o - 1], to_z(o)) for o in (4, 3, 5, 2, 6, 1, 7)])
     flush(before)
     for copy in last_t:
         copy.wait_recv()
     out_t[...] = (s.xt[slot] + sum(s.xt_r[j] for j in range(7)))[0:18]
-    for copy in last_i:
-        copy.wait_recv()
-    out_i[...] = s.zi[z] + sum(s.zi_r[j].astype(F32) for j in range(7))[0:24]
+    for (span, _, _, _, zi_r), copies in zip(sides, last_i):
+        for copy in copies:
+            copy.wait_recv()
+        out_i[:, span] = s.zi[z, :, span] + sum(zi_r[j].astype(F32) for j in range(7))[0:24]
     flush(len(started))
 
 
 def body(image_feats, text_feats, image_head, text_head, log_temp, logit_bias):
     vmem = pl.BlockSpec(memory_space=pltpu.VMEM)
-    smem = pl.BlockSpec(memory_space=pltpu.SMEM)
     anywhere = pl.BlockSpec(memory_space=pl.ANY)
     scratch = scratch_of()
 
@@ -486,7 +503,7 @@
     found = pl.pallas_call(
         run,
         out_shape=(jax.ShapeDtypeStruct((24, W), F32), jax.ShapeDtypeStruct((18, W), F32)),
-        in_specs=[anywhere, anywhere, anywhere, anywhere, smem, smem],
+        in_specs=[anywhere] * 6,
         out_specs=(vmem, vmem),
         scratch_shapes=list(scratch.values()),
         compiler_params=pltpu.CompilerParams(

time: 93.7 us -> 91.3 us (0.974)
  Pallas kernels: 91.6 us -> 88.4 us
    pallas_call x1, Pallas kernels: 90.1 us -> 87 us  [body(): pl.pallas_call(run, out_shape=(jax.ShapeDtypeStruct((24, W), F32), jax.Sh...]
where the time goes in v4:
time: 91.3 us; the launch traced here: 90.3 us
  Pallas kernels  88.4 us (97%)
  between operations  1.93 us (2%)
    pallas_call x1, Pallas kernels, body(): pl.pallas_call(run, out_shape=(jax.ShapeDtypeStruct((24, W), F32), jax.Sh...  87 us

profile of v4, /device:TPU:1, one launch (start us, length us, event | category | flops | bytes accessed | tf_op | source)
XLA Modules:
  0.0 90.3 jit_solution(3225640855447536919)
XLA Ops:
  1.9 87.0 %pair_loss.1 = (f32[24,384]{1,0:T(8,128)}, f32[18,384]{1,0:T(8,128)}) custom-call(bf16[136,1536]{1,0:T(8,128)(2,1)} %refs_0_.1, bf16[136,1152]{1,0:T(8,128)(2,1)} %refs_1_.1, bf16[1536,384]{1,0:T(8,128)(2,1)} %refs_2_.1, bf16[1152,384]{1,0:T(8,128)(2,1)} %refs_3_.1, f32[1]{0:T(128)S(6)} %copy.8.refs_4_, f32[1]{0:T(128)S(6)} %copy.9.refs_5_), custom_call_target="tpu_custom_call" | custom-call | tf_op jit(solution)/shard_map/pair_loss/pallas_call | solution.py:503
  88.9 1.4 %hand_over.1 = (f32[24,384]{1,0:T(8,128)}, f32[18,384]{1,0:T(8,128)}) custom-call(f32[24,384]{1,0:T(8,128)} %get-tuple-element.4.a, f32[18,384]{1,0:T(8,128)} %get-tuple-element.5.b), custom_call_target="tpu_custom_call" | custom-call | tf_op jit(solution)/shard_map/hand_over/pallas_call | solution.py:519

commit v5 on v2

--- a/solution.py
+++ b/solution.py
@@ -18,7 +18,7 @@
 RI = 80
 W = 384
 MESSAGES = 200
-RA, RB = 64, 80
+RA, RB = 80, 64
 I_CHUNKS = ((0, (0, 48)), (0, (48, 32)), (1, (0, 48)), (1, (48, 32)))
 T_CHUNKS = ((0, 32), (32, 32), (64, 32), (96, 48))
 
@@ -44,8 +44,8 @@
         a1=bf16(3, 2, RA, 2 * W), a_sum=f32(2, RA, 2 * W), a_s=bf16(2, RA, 2 * W), a2=bf16(3, RA, W),
         b1=bf16(3, 4, RB, W), b_sum=f32(4, RB, W), b_s=bf16(4, RB, W), b2=bf16(3, RB, W),
         swap_s=bf16(RI, W), swap_r=bf16(RI, W), both=f32(2, RI, W), t_sum=f32(RT, W),
-        head_t=f32(1152, W), head_i=f32(1536, W), si=bf16(8, 192, W), ri=bf16(7, 192, W),
-        zi=f32(8, 24, W), zi_s=bf16(8, 32, W), zi_r=bf16(7, 32, W), xt=f32(8, 24, W), xt_r=f32(7, 24, W),
+        head_t=f32(1152, W), head_i=f32(1536, W), si0=bf16(8, 192, 256), ri0=bf16(7, 192, 256), si1=bf16(8, 192, 128), ri1=bf16(7, 192, 128),
+        zi=f32(8, 24, W), zi_s0=bf16(8, 32, 256), zi_r0=bf16(7, 32, 256), zi_s1=bf16(8, 32, 128), zi_r1=bf16(7, 32, 128), xt=f32(8, 24, W), xt_r=f32(7, 24, W),
     )
 
     def ring(name, steps, *shapes):
@@ -113,6 +113,13 @@
         copy.start()
         started.append(copy)
         return copy
+
+    flushed = [0]
+
+    def flush(upto):
+        for copy in started[flushed[0] : upto]:
+            copy.wait_send()
+        flushed[0] = max(upto, flushed[0])
 
     def lanes(half):
         return pl.ds(pl.multiple_of(half * W, 128), W)
@@ -310,6 +317,7 @@
     share_a = pairs("a", RA, 0, cross_a)
     for copy in go_b2:
         copy.wait_recv()
+    arrived = len(started)
     cross_b = products("b", RB)
     share_a.wait_recv()
     text_grads("a", RA)
@@ -346,6 +354,7 @@
     next(back_z)
     s.swap_s[...] = s.grad_i[z, :, kinds[1]].astype(BF16)
     swap_back = message(s.swap_s, s.swap_r, to_x(2))
+    flush(arrived)
     next(back_z)
     next(back_z)
     for copy in back_a1:
@@ -355,16 +364,17 @@
     back_a2 = [
         message(s.a_s.at[lax.rem(xo(o), 2), :, lanes(lax.div(xo(o), 2))], s.a2.at[o - 1], to_x(o)) for o in (1, 2, 3)
     ]
-    next(back_z)
     for copy in back_b1:
         copy.wait_recv()
     s.b_sum[...] = s.grad_b[xl, :, :, own] + sum(s.b1[o].astype(F32) for o in range(3))
     s.b_s[...] = s.b_sum[...].astype(BF16)
     back_b2 = [message(s.b_s.at[yo(o)], s.b2.at[o - 1], to_y(o)) for o in (1, 2, 3)]
     next(back_z)
+    next(back_z)
     swap_back.wait_recv()
     s.both[1 - xh] += s.swap_r[...].astype(F32)
     img_unit_grad = jnp.concatenate([s.both[0, pl.ds(0, 64)], s.both[1]], axis=0)
+    returned = len(started)
     sent_i = send_sums(s.along_i, img_unit_grad * s.dir_i[...])()
     for copy in back_a2:
         copy.wait_recv()
@@ -378,8 +388,10 @@
     img_unit_grad = jnp.concatenate([s.both[0, pl.ds(0, 64)], s.both[1]], axis=0)
     img_grad = ((img_unit_grad - s.dir_i[...] * along[:, 0:1]) / s.norm_i[:, 0:1]).astype(BF16)
     s.head_i[...] = lax.dot_general(s.xf[...], img_grad[0:R], TN, preferred_element_type=F32)
-    for j in range(8):
-        s.si[j] = jnp.concatenate([s.head_i[pl.ds(k * 192 + j * 24, 24), :] for k in range(8)], axis=0).astype(BF16)
+    sides = ((pl.ds(0, 256), s.si0, s.ri0, s.zi_s0, s.zi_r0), (pl.ds(256, 128), s.si1, s.ri1, s.zi_s1, s.zi_r1))
+    for span, si, _, _, _ in sides:
+        for j in range(8):
+            si[j] = jnp.concatenate([s.head_i[pl.ds(k * 192 + j * 24, 24), span] for k in range(8)], axis=0).astype(BF16)
 
     def over_xy(src, dst):
         copies = []
@@ -391,7 +403,7 @@
                     copies.append(message(src.at[to_xl * 4 + yo(b)], dst.at[a * 4 + b - 1], where))
         return copies
 
-    fore_i = over_xy(s.si, s.ri)
+    fore_i = [over_xy(si, ri) for _, si, ri, _, _ in sides]
     along = sums_of(s.along_t, sent_t)
     txt_grad = ((s.t_sum[...] - s.dir_t[...] * along[:, 0:1]) / s.norm_t[:, 0:1]).astype(BF16)
     s.head_t[...] = lax.dot_general(s.tf[...], txt_grad[0:R], TN, preferred_element_type=F32)
@@ -404,30 +416,37 @@
 
     fore_t = reduce("ht", text_term, to_z, 8, text_done, 4)
     next(fore_t)
+    flush(returned)
     next(fore_t)
     next(fore_t)
     next(fore_t)
-    for copy in fore_i:
-        copy.wait_recv()
-    for k in range(8):
-        s.zi[k] = s.head_i[pl.ds(pl.multiple_of(k * 192 + slot * 24, 8), 24), :]
-    s.zi[...] += sum(s.ri[j].astype(F32) for j in range(7)).reshape(8, 24, W)
-    for k in range(8):
-        s.zi_s[k] = padded(s.zi[k], 32).astype(BF16)
-    last_i = [message(s.zi_s.at[zo(o)], s.zi_r.at[o - 1], to_z(o)) for o in (4, 3, 5, 2, 6, 1, 7)]
-    next(fore_t)
-    total = s.t_sum[...]
-    for j in range(8):
-        s.xt[j] = padded(total[18 * j : 18 * j + 18], 24)
-    last_t = over_xy(s.xt, s.xt_r)
+    last_i = []
+    for side, (span, _, ri, zi_s, zi_r) in enumerate(sides):
+        if side == 1:
+            next(fore_t)
+            before = len(started)
+            total = s.t_sum[...]
+            for j in range(8):
+                s.xt[j] = padded(total[18 * j : 18 * j + 18], 24)
+            last_t = over_xy(s.xt, s.xt_r)
+        for copy in fore_i[side]:
+            copy.wait_recv()
+        whole = sum(ri[j].astype(F32) for j in range(7))
+        for k in range(8):
+            s.zi[k, :, span] = (
+                s.head_i[pl.ds(pl.multiple_of(k * 192 + slot * 24, 8), 24), span] + whole[k * 24 : k * 24 + 24]
+            )
+            zi_s[k] = padded(s.zi[k, :, span], 32).astype(BF16)
+        last_i.append([message(zi_s.at[zo(o)], zi_r.at[o - 1], to_z(o)) for o in (4, 3, 5, 2, 6, 1, 7)])
+    flush(before)
     for copy in last_t:
         copy.wait_recv()
     out_t[...] = (s.xt[slot] + sum(s.xt_r[j] for j in range(7)))[0:18]
-    for copy in last_i:
-        copy.wait_recv()
-    out_i[...] = s.zi[z] + sum(s.zi_r[j].astype(F32) for j in range(7))[0:24]
-    for copy in started:
-        copy.wait_send()
+    for (span, _, _, _, zi_r), copies in zip(sides, last_i):
+        for copy in copies:
+            copy.wait_recv()
+        out_i[:, span] = s.zi[z, :, span] + sum(zi_r[j].astype(F32) for j in range(7))[0:24]
+    flush(len(started))
 
 
 def body(image_feats, text_feats, image_head, text_head, log_temp, logit_bias):
@@ -439,7 +458,7 @@
     def run(*refs):
         kernel(tuple(scratch), *refs)
 
-    return pl.pallas_call(
+    found = pl.pallas_call(
         run,
         out_shape=(jax.ShapeDtypeStruct((24, W), F32), jax.ShapeDtypeStruct((18, W), F32)),
         in_specs=[anywhere, anywhere, anywhere, anywhere, smem, smem],
@@ -451,6 +470,18 @@
         name="pair_loss",
     )(image_feats, text_feats, image_head, text_head, log_temp, logit_bias)
 
+    def hand_over(a, b, c, d):
+        c[...] = a[...]
+        d[...] = b[...]
+
+    return pl.pallas_call(
+        hand_over,
+        out_shape=(jax.ShapeDtypeStruct((24, W), F32), jax.ShapeDtypeStruct((18, W), F32)),
+        in_specs=[vmem, vmem],
+        out_specs=(vmem, vmem),
+        name="hand_over",
+    )(*found)
+
 
 def solution(mesh):
     placed = (P("dp", None), P("dp", None), P(None, "mp"), P(None, "mp"), P(), P())

time: 97.8 us -> 93.7 us (0.958)
  local copies, waits for them, and re-layouts: 2.77 us -> 0 us
  Pallas kernels: 92.8 us -> 91.1 us
    pallas_call x1, Pallas kernels: 92.8 us -> 89.6 us  [body(): pl.pallas_call(run, out_shape=(jax.ShapeDtypeStruct((24, W), F32), jax.Sh...]
    unnamed x2 -> x0, local copies, waits for them, and re-layouts: 2.77 us -> none
    pallas_call x0 -> x1, Pallas kernels: none -> 1.42 us  [body(): pl.pallas_call(hand_over, out_shape=(jax.ShapeDtypeStruct((24, W), F32),...]
where the time goes in v5:
time: 93.7 us; the launch traced here: 93 us
  Pallas kernels  91.1 us (97%)
  between operations  1.93 us (2%)
    pallas_call x1, Pallas kernels, body(): pl.pallas_call(run, out_shape=(jax.ShapeDtypeStruct((24, W), F32), jax.Sh...  89.6 us

profile of v5, /device:TPU:1, one launch (start us, length us, event | category | flops | bytes accessed | tf_op | source)
XLA Modules:
  0.0 93.0 jit_solution(2795245159885832037)
XLA Ops:
  1.9 89.6 %pair_loss.1 = (f32[24,384]{1,0:T(8,128)}, f32[18,384]{1,0:T(8,128)}) custom-call(bf16[136,1536]{1,0:T(8,128)(2,1)} %refs_0_.1, bf16[136,1152]{1,0:T(8,128)(2,1)} %refs_1_.1, bf16[1536,384]{1,0:T(8,128)(2,1)} %refs_2_.1, bf16[1152,384]{1,0:T(8,128)(2,1)} %refs_3_.1, f32[1]{0:T(128)S(6)} %copy.8.refs_4_, f32[1]{0:T(128)S(6)} %copy.9.refs_5_), custom_call_target="tpu_custom_call" | custom-call | tf_op jit(solution)/shard_map/pair_loss/pallas_call | solution.py:461
  91.6 1.4 %hand_over.1 = (f32[24,384]{1,0:T(8,128)}, f32[18,384]{1,0:T(8,128)}) custom-call(f32[24,384]{1,0:T(8,128)} %get-tuple-element.4.a, f32[18,384]{1,0:T(8,128)} %get-tuple-element.5.b), custom_call_target="tpu_custom_call" | custom-call | tf_op jit(solution)/shard_map/hand_over/pallas_call | solution.py:477
